TPU v7x, 256 devices: a whole 4x4x8 slice. The times are simulated.
256 devices in a mesh: grp: 8 (over z), row: 32 (over x, y, core).
Axes of the slice: x: 4, y: 4, z: 8, core: 2. Of those that a mesh axis runs over, the one named last changes fastest.
Arguments:
- operator: bfloat16 [4096, 16, 128, 128], P(('grp', 'row')), may hold values from -0.125 to 0.125
- columns: int32 [4096, 16], P(('grp', 'row')), may hold values from 0 to 4095, as said below
- live_blocks: int32 [4096], P(('grp', 'row')), may hold values from 1 to 16, as said below
- viscosity: float32 [4096], P(('grp', 'row')), may hold values from 0.001 to 3
- sketch: bfloat16 [524288, 128], P(('grp', 'row')), may hold values from -6 to 6
Outputs:
- basis: float32 [524288, 128], P(('grp', 'row'))
- triangle: float32 [128, 128], replicated
Inputs may be any that keep to these rules, and one draw needn't show every extreme that they name: Block row r of the device with linear index d (grp slowest) names only block columns of devices d - 1, d and d + 1, that is (d - 1) * 16 to (d + 2) * 16 - 1, within the slab. `live_blocks`: block row 0 has all 16 slots live.
All inputs are finite; a program needn't handle non-finite values.
Results may differ from a plain program's by a relative error of at most 0.0003.
Values may be sent and summed in bfloat16 or wider, within the bound.
A program may use at most 64 MiB of HBM per device.

v0:
```python
import jax
import jax.numpy as jnp
from jax import lax
from jax.sharding import PartitionSpec as P


def extended(x, sides, width):
    for axis, dim in sides:
        peers, length = (lax.axis_size(axis), x.shape[dim])
        up = [(i, (i + 1) % peers) for i in range(peers - 1)]
        down = [(j, i) for i, j in up]
        last = lax.slice_in_dim(x, length - width, length, axis=dim)
        initial = lax.slice_in_dim(x, 0, width, axis=dim)
        before = lax.ppermute(last, axis, up)
        after = lax.ppermute(initial, axis, down)
        x = jnp.concatenate([before, x, after], axis=dim)
    return x


def shards(operator, columns, live_blocks, viscosity, sketch):
    rows_dev, width = sketch.shape
    blocks, slots, bsize = (operator.shape[0], operator.shape[1], operator.shape[2])
    device = lax.axis_index("grp") * lax.axis_size("row") + lax.axis_index("row")
    local_cols = columns - (device - 1) * blocks
    keep = jnp.arange(slots, dtype=jnp.int32)[None, :] < live_blocks[:, None]
    window = extended(sketch, ((("grp", "row"), 0),), rows_dev)
    window = window.reshape(3 * blocks, bsize, width)
    picked = window[local_cols]
    picked = jnp.where(keep[:, :, None, None], picked, jnp.zeros((), jnp.bfloat16))
    product = jnp.einsum("rnij,rnjk->rik", operator, picked, preferred_element_type=jnp.float32)
    image = (product * viscosity[:, None, None]).reshape(rows_dev, width)
    partial_gram = jnp.dot(image.T, image, precision=lax.Precision.HIGHEST)
    gram = lax.psum(partial_gram, ("grp", "row"))
    total_rows = rows_dev * lax.axis_size("grp") * lax.axis_size("row")
    gram = gram / jnp.float32(total_rows)
    lower = jnp.linalg.cholesky(gram)
    basis = jax.scipy.linalg.solve_triangular(lower, image.T, lower=True).T
    return (basis, lower.T)


def solution(mesh):
    return jax.shard_map(
        shards,
        mesh=mesh,
        in_specs=(
            P(("grp", "row"), None, None, None),
            P(("grp", "row"), None),
            P(("grp", "row")),
            P(("grp", "row")),
            P(("grp", "row"), None),
        ),
        out_specs=(P(("grp", "row"), None), P()),
        check_vma=False,
    )
```

profile of v0, /device:TPU:1, one launch (start us, length us, event | category | flops | bytes accessed | tf_op | source)
XLA Modules:
  0.0 321.3 jit_solution(1740933710100136216)
XLA Ops:
  7.2 0.0 all-reduce.2.cloned.1.call-start
  7.2 4.6 %collective-permute-start = (bf16[2048,128]{1,0:T(8,128)(2,1)}, bf16[2048,128]{1,0:T(8,128)(2,1)S(1)}, u32[]{:S(2)}, u32[]{:S(2)}) collective-permute-start(bf16[2048,128]{1,0:T(8,128)(2,1)} %param.9), channel_id=1, source_target_pairs={{0,1},{1,2},{2,3},{3,4},{4,5},{5,6},{6,7},{7,8},{8,9},{9,10},{10,1... | collective-permute-start | bytes 1572872 | tf_op jit(solution)/shard_map/ppermute | solution.py:14
  11.8 1.9 collective-permute-start.1
  13.8 0.7 compare_select_fusion
  14.5 0.1 reshape.46
  14.5 0.7 iota_compare_fusion.2
  15.3 3.0 collective-permute-done
  18.2 4.3 %collective-permute-done.1 = bf16[2048,128]{1,0:T(8,128)(2,1)S(1)} collective-permute-done((bf16[2048,128]{1,0:T(8,128)(2,1)}, bf16[2048,128]{1,0:T(8,128)(2,1)S(1)}, u32[]{:S(2)}, u32[]{:S(2)}) %collective-permute-start.1) | collective-permute-done | bytes 524320 | tf_op jit(solution)/shard_map/ppermute | solution.py:15
  22.5 1.1 pad_maximum_fusion
  23.7 0.0 copy-start
  23.7 8.6 %gather_fusion = bf16[256,128,128]{2,1,0:T(8,128)(2,1)} fusion(bf16[48,128,128]{2,1,0:T(8,128)(2,1)S(1)} %bitcast.27, s32[1024]{0:T(1024)S(1)} %pad_clamp_fusion), kind=kCustom, calls=%fused_computation | custom fusion | bytes 16778240 | tf_op jit(solution)/shard_map/gather | solution.py:28
  32.3 0.0 copy-done
  32.3 8.2 %fusion.7 = f32[16,128,128]{1,2,0:T(8,128)S(1)} fusion(bf16[16,16,128,128]{3,2,1,0:T(8,128)(2,1)} %param.5, bf16[16,16,128,128]{3,2,1,0:T(8,128)(2,1)} %bitcast.28, pred[16,16]{1,0:T(8,128)(4,1)S(1)} %iota_compare_fusion.2, f32[16]{0:T(128)S(1)} %copy-done), kind=kOutput, calls=%fused_computation.7 | convolution fusion | flops 1078198272 | bytes 17826112 | tf_op jit(solution)/shard_map/rnij,rnjk->rik/dot_general | solution.py:30
  40.5 2.4 convolution_bitcast_fusion
  42.9 0.0 all-reduce.2.cloned.1.call-update
  43.0 244.2 %all-reduce.2.cloned.1.call-done = f32[128,128]{0,1:T(8,128)} async-done(((f32[128,128]{0,1:T(8,128)}), f32[128,128]{0,1:T(8,128)}) %all-reduce.2.cloned.1.call-update) | async-done | bytes 65552 | tf_op jit(solution)/shard_map/psum | solution.py:33
  287.1 0.8 broadcast_multiply_fusion
  288.0 0.1 copy.9
  288.1 0.9 fusion.13
  288.9 11.7 %cholesky.16 = f32[128,128]{1,0:T(8,128)S(1)} custom-call(f32[128,128]{1,0:T(8,128)S(1)} %fusion.13), custom_call_target="Cholesky" | custom-call | tf_op jit(solution)/shard_map/jit(cholesky)/cholesky | solution.py:36
  300.7 0.6 compare_reduce_fusion
  301.3 0.7 fusion.14
  302.0 9.8 %custom-call.7 = f32[1,128,128]{1,2,0:T(8,128)S(1)} custom-call(f32[1,128,128]{2,1,0:T(8,128)S(1)} %get-tuple-element.5), custom_call_target="InvertDiagBlocksLowerTriangular" | custom-call | tf_op jit(solution)/shard_map/jit(_solve_triangular)/triangular_solve | solution.py:37
  311.8 0.7 copy.10
  312.5 1.9 fusion.11
  (2 shorter events, 0.0 us)
Async XLA Ops:
  7.2 280.0 %all-reduce.2.cloned.1.call-start = ((), (), s32[]{:S(2)}) async-start(), calls=%async_computation | async-start | bytes 131072 | tf_op jit(solution)/shard_map/psum | solution.py:33
  7.2 11.0 %collective-permute-start = (bf16[2048,128]{1,0:T(8,128)(2,1)}, bf16[2048,128]{1,0:T(8,128)(2,1)S(1)}, u32[]{:S(2)}, u32[]{:S(2)}) collective-permute-start(bf16[2048,128]{1,0:T(8,128)(2,1)} %param.9), channel_id=1, source_target_pairs={{0,1},{1,2},{2,3},{3,4},{4,5},{5,6},{6,7},{7,8},{8,9},{9,10},{10,1... | collective-permute-start | bytes 1572872 | tf_op jit(solution)/shard_map/ppermute | solution.py:14
  11.8 10.7 %collective-permute-start.1 = (bf16[2048,128]{1,0:T(8,128)(2,1)}, bf16[2048,128]{1,0:T(8,128)(2,1)S(1)}, u32[]{:S(2)}, u32[]{:S(2)}) collective-permute-start(bf16[2048,128]{1,0:T(8,128)(2,1)} %param.9), channel_id=1, source_target_pairs={{1,0},{2,1},{3,2},{4,3},{5,4},{6,5},{7,6},{8,7},{9,8},{10,9},{11,1... | collective-permute-start | bytes 1572872 | tf_op jit(solution)/shard_map/ppermute | solution.py:15
  23.7 8.6 %copy-start = (f32[16]{0:T(128)S(1)}, f32[16]{0:T(128)}, u32[]{:S(2)}) copy-start(f32[16]{0:T(128)} %param.8) | copy-start | bytes 196
Sparse Core Ops, SparseCore 0:
  43.1 243.9 all-reduce.1
where the time goes:
time: 322 us; the launch traced here: 321 us
  waiting for transfers between devices  251 us (78%)
  other arithmetic  27.1 us (8%)
  between operations  14.1 us (4%)
  matrix products  12.6 us (4%)
  local copies, waits for them, and re-layouts  9.52 us (3%)
  starting transfers between devices  6.56 us (2%)
    psum x1, waiting for transfers between devices, shards(): gram = lax.psum(partial_gram, ('grp', 'row'))  244 us
    another operation x3, other arithmetic, shards(): lower = jnp.linalg.cholesky(gram)  12.4 us
    another operation x1, other arithmetic, shards(): basis = jax.scipy.linalg.solve_triangular(lower, image.T, lower=True).T  9.81 us
    gather x1, local copies, waits for them, and re-layouts, shards(): picked = window[local_cols]  8.61 us
    dot_general x1, matrix products, shards(): jnp.einsum('rnij,rnjk->rik', operator, picked, preferred_element_type=jnp...  8.18 us
  transfers between devices with their start and end apart: 3, of which 3 were waited for; matrix products, arithmetic and copies ran while one was open for 0% of the time, Pallas kernels for 0%

commit v1 on v0

v1 whole, which is shorter than its diff:
```python
import jax
import jax.numpy as jnp
from jax import lax
from jax.experimental import pallas as pl
from jax.experimental.pallas import tpu as pltpu
from jax.sharding import PartitionSpec as P

MESH = pl.DeviceIdType.MESH
F32 = jnp.float32
BF16 = jnp.bfloat16

GRP, ROW = 8, 32
NDEV = GRP * ROW
BLOCKS = 16
SLOTS = 16
B = 128
K = 128
LINE = 16
PLANE = 16
SUB = 8
DEAD = 3 * BLOCKS


def remote(src, dst, send_sem, recv_sem, device):
    return pltpu.make_async_remote_copy(
        src_ref=src, dst_ref=dst, send_sem=send_sem, recv_sem=recv_sem, device_id=device, device_id_type=MESH
    )


def lanes(v, c):
    return jnp.broadcast_to(v[:, c : c + 1], (SUB, K))


def rows(v, i):
    return jnp.broadcast_to(v[i : i + 1, :], (SUB, K))


def factor(gram, tri_ref, inv_ref):
    lane = lax.broadcasted_iota(jnp.int32, (SUB, K), 1)
    sub = lax.broadcasted_iota(jnp.int32, (SUB, K), 0)
    n = K // SUB
    a = list(gram)
    x = [jnp.where(lane == sub + SUB * q, 1.0, 0.0).astype(F32) for q in range(n)]
    for p in range(n):
        o = SUB * p
        col = {q: [lanes(a[q], o + k) for k in range(SUB)] for q in range(p, n)}
        diag = [[rows(col[p][j], i) if j <= i else None for j in range(SUB)] for i in range(SUB)]
        ra = [rows(a[p], i) for i in range(SUB)]
        rx = [rows(x[p], i) for i in range(SUB)]
        inv = [None] * SUB
        for k in range(SUB):
            inv[k] = 1.0 / diag[k][k]
            mult = {i: diag[i][k] * inv[k] for i in range(k + 1, SUB)}
            for i in range(k + 1, SUB):
                for j in range(k + 1, i + 1):
                    diag[i][j] = diag[i][j] - mult[i] * diag[j][k]
            for i in range(k + 1, SUB):
                ra[i] = ra[i] - mult[i] * ra[k]
                rx[i] = rx[i] - mult[i] * rx[k]
            for q in range(p + 1, n):
                for i in range(k + 1, SUB):
                    col[q][i] = col[q][i] - mult[i] * col[q][k]
        for i in range(SUB):
            root = lax.rsqrt(diag[i][i])
            tri_ref[o + i : o + i + 1, :] = jnp.where(lane >= o + i, ra[i] * root, 0.0)[0:1]
            inv_ref[o + i : o + i + 1, :] = (rx[i] * root)[0:1]
        ga = [ra[i] * inv[i] for i in range(SUB)]
        gx = [rx[i] * inv[i] for i in range(SUB)]
        for q in range(p + 1, n):
            for k in range(SUB):
                a[q] = a[q] - col[q][k] * ga[k]
                x[q] = x[q] - col[q][k] * gx[k]


def split3(v):
    hi = v.astype(BF16)
    rest = v - hi.astype(F32)
    mid = rest.astype(BF16)
    low = (rest - mid.astype(F32)).astype(BF16)
    return hi, mid, low


def kernel(
    cols_ref, live_ref, visc_ref, op_hbm, sketch_hbm, basis_hbm, tri_ref,
    ops, window, image, gram, part, recv1, recv2, total, inverse, out,
    op_sems, own_sem, out_sems, halo_send, halo_recv, send_sems, recv_sems,
):
    z, row = lax.axis_index("grp"), lax.axis_index("row")
    core = lax.rem(row, 2)
    chip = row // 2
    me = z * ROW + row
    mine = 2 * z + core

    loads = []
    for r in range(BLOCKS):
        loads.append(pltpu.make_async_copy(op_hbm.at[r], ops.at[r], op_sems.at[r]))
    own = pltpu.make_async_copy(sketch_hbm, window.at[pl.ds(BLOCKS, BLOCKS)], own_sem)

    def line_peer(k):
        other = lax.rem(mine + k, LINE)
        return other, (other // 2, row - core + lax.rem(other, 2))

    def plane_peer(k):
        other = lax.rem(chip + k, PLANE)
        return other, (z, other * 2 + core)

    order = sorted(range(1, LINE), key=lambda k: -min(k, LINE - k))
    up = lax.rem(me + 1, NDEV)
    down = lax.rem(me + NDEV - 1, NDEV)
    up_dev = (up // ROW, lax.rem(up, ROW))
    down_dev = (down // ROW, lax.rem(down, ROW))

    barrier = pltpu.get_barrier_semaphore()
    peers = [up_dev, down_dev] + [line_peer(k)[1] for k in order] + [plane_peer(k)[1] for k in order]
    for dev in peers:
        pl.semaphore_signal(barrier, inc=1, device_id=dev, device_id_type=MESH)
    own.start()
    for c in loads:
        c.start()
    window[DEAD] = jnp.zeros((B, K), BF16)
    pl.semaphore_wait(barrier, len(peers))

    halo = [
        remote(sketch_hbm, window.at[pl.ds(0, BLOCKS)], halo_send.at[0], halo_recv.at[0], up_dev),
        remote(sketch_hbm, window.at[pl.ds(2 * BLOCKS, BLOCKS)], halo_send.at[1], halo_recv.at[1], down_dev),
    ]
    for c in halo:
        c.start()
    own.wait()
    for c in loads:
        c.wait()
    for c in halo:
        c.wait()

    base = (me - 1) * BLOCKS
    gram[...] = jnp.zeros_like(gram)

    def block_row(r, _):
        live = live_ref[r]
        acc = jnp.zeros((B, K), F32)
        for s in range(0, SLOTS, 2):
            i0 = jnp.where(s < live, cols_ref[r, s] - base, DEAD)
            i1 = jnp.where(s + 1 < live, cols_ref[r, s + 1] - base, DEAD)
            lhs = jnp.concatenate([ops[r, s], ops[r, s + 1]], axis=1)
            rhs = jnp.concatenate([window[i0], window[i1]], axis=0)
            acc = acc + jnp.dot(lhs, rhs, preferred_element_type=F32)
        img = acc * visc_ref[r]
        image[pl.ds(pl.multiple_of(r * B, B), B), :] = img
        hi, mid, low = split3(img)
        first = lax.dot_general(
            hi, jnp.concatenate([hi, mid, low], axis=1), (((0,), (0,)), ((), ())), preferred_element_type=F32
        )
        second = lax.dot_general(mid, mid, (((0,), (0,)), ((), ())), preferred_element_type=F32)
        gram[:, 0:K] += first[:, 0:K] + second
        gram[:, K : 2 * K] += first[:, K : 2 * K] + first[:, 2 * K :]
        return 0

    lax.fori_loop(0, BLOCKS, block_row, 0)
    cross = gram[:, K : 2 * K]
    local = gram[:, 0:K] + (cross + cross.T)
    part[...] = local.reshape(LINE, SUB, K)

    recv1[mine] = part[mine]
    copies = []
    for k in order:
        other, dev = line_peer(k)
        c = remote(part.at[other], recv1.at[mine], send_sems.at[0, other], recv_sems.at[0, mine], dev)
        c.start()
        copies.append(c)
    for k in order:
        other, dev = line_peer(k)
        remote(part.at[other], recv1.at[other], send_sems.at[0, other], recv_sems.at[0, other], dev).wait_recv()
    mine_sum = jnp.sum(recv1[...], axis=0)
    recv2[chip] = mine_sum
    for k in order:
        other, dev = plane_peer(k)
        c = remote(recv2.at[chip], recv2.at[chip], send_sems.at[1, other], recv_sems.at[1, chip], dev)
        c.start()
        copies.append(c)
    for k in order:
        other, dev = plane_peer(k)
        remote(recv2.at[other], recv2.at[other], send_sems.at[1, other], recv_sems.at[1, other], dev).wait_recv()
    total[mine] = jnp.sum(recv2[...], axis=0)
    for k in order:
        other, dev = line_peer(k)
        c = remote(total.at[mine], total.at[mine], send_sems.at[2, other], recv_sems.at[2, mine], dev)
        c.start()
        copies.append(c)
    for k in order:
        other, dev = line_peer(k)
        remote(total.at[other], total.at[other], send_sems.at[2, other], recv_sems.at[2, other], dev).wait_recv()

    scale = 1.0 / (NDEV * BLOCKS * B)
    factor([total[q] * scale for q in range(K // SUB)], tri_ref, inverse)

    whi, wmid, wlow = split3(inverse[...])
    weights = jnp.concatenate([whi, whi, wmid, whi, wmid, wlow], axis=1)

    def basis_row(r, _):
        at = pl.ds(pl.multiple_of(r * B, B), B)
        hi, mid, low = split3(image[at, :])
        lhs = jnp.concatenate([hi, mid, hi, low, mid, hi], axis=1)
        out[at, :] = lax.dot_general(lhs, weights, (((1,), (1,)), ((), ())), preferred_element_type=F32)
        pltpu.make_async_copy(out.at[at], basis_hbm.at[at], out_sems.at[r]).start()
        return 0

    lax.fori_loop(0, BLOCKS, basis_row, 0)
    for r in range(BLOCKS):
        at = pl.ds(r * B, B)
        pltpu.make_async_copy(out.at[at], basis_hbm.at[at], out_sems.at[r]).wait()
    for c in copies:
        c.wait_send()


def shards(operator, columns, live_blocks, viscosity, sketch):
    rows_dev = BLOCKS * B
    smem = pl.BlockSpec(memory_space=pltpu.SMEM)
    hbm = pl.BlockSpec(memory_space=pl.ANY)
    return pl.pallas_call(
        kernel,
        out_shape=[jax.ShapeDtypeStruct((rows_dev, K), F32), jax.ShapeDtypeStruct((K, K), F32)],
        in_specs=[smem, smem, smem, hbm, hbm],
        out_specs=[hbm, pl.BlockSpec(memory_space=pltpu.VMEM)],
        scratch_shapes=[
            pltpu.VMEM((BLOCKS, SLOTS, B, B), BF16),
            pltpu.VMEM((3 * BLOCKS + 1, B, K), BF16),
            pltpu.VMEM((rows_dev, K), F32),
            pltpu.VMEM((K, 2 * K), F32),
            pltpu.VMEM((LINE, SUB, K), F32),
            pltpu.VMEM((LINE, SUB, K), F32),
            pltpu.VMEM((PLANE, SUB, K), F32),
            pltpu.VMEM((LINE, SUB, K), F32),
            pltpu.VMEM((K, K), F32),
            pltpu.VMEM((rows_dev, K), F32),
            pltpu.SemaphoreType.DMA((BLOCKS,)),
            pltpu.SemaphoreType.DMA,
            pltpu.SemaphoreType.DMA((BLOCKS,)),
            pltpu.SemaphoreType.DMA((2,)),
            pltpu.SemaphoreType.DMA((2,)),
            pltpu.SemaphoreType.DMA((3, LINE)),
            pltpu.SemaphoreType.DMA((3, LINE)),
        ],
        compiler_params=pltpu.CompilerParams(
            collective_id=0, has_side_effects=True, vmem_limit_bytes=48 * 2**20
        ),
        cost_estimate=pl.CostEstimate(flops=1_300_000_000, bytes_accessed=11_000_000, transcendentals=0),
    )(columns, live_blocks, viscosity, operator, sketch.reshape(BLOCKS, B, K))


def solution(mesh):
    return jax.shard_map(
        shards,
        mesh=mesh,
        in_specs=(
            P(("grp", "row"), None, None, None),
            P(("grp", "row"), None),
            P(("grp", "row")),
            P(("grp", "row")),
            P(("grp", "row"), None),
        ),
        out_specs=(P(("grp", "row"), None), P()),
        check_vma=False,
    )
```

time: 322 us -> 59.1 us (0.18)
  waiting for transfers between devices: 251 us -> 0 us
  Pallas kernels: 0 us -> 53.6 us
  other arithmetic: 27.1 us -> 0 us
  between operations: 14.1 us -> 0.65 us
  matrix products: 12.6 us -> 0 us
  starting transfers between devices: 6.56 us -> 0 us
  local copies, waits for them, and re-layouts: 9.52 us -> 4.64 us
    psum x1 -> x0, waiting for transfers between devices: 244 us -> none  [shards(): gram = lax.psum(partial_gram, ('grp', 'row'))]
    pallas_call x0 -> x1, Pallas kernels: none -> 53.6 us  [shards(): pl.pallas_call(kernel, out_shape=[jax.ShapeDtypeStruct((rows_dev, K), F32...]
    another operation x4 -> x0, other arithmetic: 22.2 us -> none  [the longest x3 12.4 us: shards(): lower = jnp.linalg.cholesky(gram)]
    dot_general x2 -> x0, matrix products: 10.6 us -> none  [the longest x1 8.18 us: shards(): jnp.einsum('rnij,rnjk->rik', operator, picked, preferred_element_type=jnp...]
    gather x1 -> x0, local copies, waits for them, and re-layouts: 8.61 us -> none  [shards(): picked = window[local_cols]]
    ppermute x2 -> x0, waiting for transfers between devices: 7.25 us -> none  [the longest x1 4.29 us: extended(): after = lax.ppermute(initial, axis, down)]
    ppermute x2 -> x0, starting transfers between devices: 6.52 us -> none  [the longest x1 4.6 us: extended(): before = lax.ppermute(last, axis, up)]
    unnamed x3 -> x10, local copies, waits for them, and re-layouts: 0.74 us -> 4.64 us
  transfers between devices with their start and end apart: 3 -> 0, of which waited for: 3 -> 0; matrix products, arithmetic and copies ran while one was open for 0% -> 0% of each run, Pallas kernels for 0% -> 0%
where the time goes in v1:
time: 59.1 us; the launch traced here: 58.9 us
  Pallas kernels  53.6 us (91%)
  local copies, waits for them, and re-layouts  4.64 us (8%)
  between operations  0.65 us (1%)
    pallas_call x1, Pallas kernels, shards(): pl.pallas_call(kernel, out_shape=[jax.ShapeDtypeStruct((rows_dev, K), F32...  53.6 us
    unnamed x10, local copies, waits for them, and re-layouts  4.64 us

profile of v1, /device:TPU:1, one launch (start us, length us, event | category | flops | bytes accessed | tf_op | source)
XLA Modules:
  0.0 58.9 jit_solution(7145195789363952342)
XLA Ops:
  0.6 0.0 copy-start
  0.6 1.0 %copy-done = bf16[2048,128]{1,0:T(8,128)(2,1)S(1)} copy-done((bf16[2048,128]{1,0:T(8,128)(2,1)S(1)}, bf16[2048,128]{1,0:T(8,128)(2,1)}, u32[]{:S(2)}) %copy-start) | copy-done | bytes 524312
  1.7 0.0 copy-start.1
  1.7 0.7 %copy-done.1 = s32[16,16]{1,0:T(8,128)S(1)} copy-done((s32[16,16]{1,0:T(8,128)S(1)}, s32[16,16]{1,0:T(8,128)}, u32[]{:S(2)}) %copy-start.1) | copy-done | bytes 1048
  2.4 0.0 copy-start.2
  2.4 0.7 %copy-done.2 = s32[16]{0:T(128)S(1)} copy-done((s32[16]{0:T(128)S(1)}, s32[16]{0:T(128)}, u32[]{:S(2)}) %copy-start.2) | copy-done | bytes 88
  3.0 0.0 copy-start.3
  3.0 0.7 %copy-done.3 = f32[16]{0:T(128)S(1)} copy-done((f32[16]{0:T(128)S(1)}, f32[16]{0:T(128)}, u32[]{:S(2)}) %copy-start.3) | copy-done | bytes 88
  3.7 53.6 %shard_map.68 = (f32[2048,128]{1,0:T(8,128)S(1)}, f32[128,128]{1,0:T(8,128)S(1)}) custom-call(s32[16,16]{1,0:T(8,128)S(1)} %copy-done.1, s32[16]{0:T(128)S(1)} %copy-done.2, f32[16]{0:T(128)S(1)} %copy-done.3, bf16[16,16,128,128]{3,2,1,0:T(8,128)(2,1)} %op_hbm.1, bf16[16,128,128]{2,1,0:T(8,128)(2,1)S(1)} %bitcast.1), custom_call_target="tpu_custom_call" | custom-call | flops 1300000000 | bytes 11000000 | tf_op jit(solution)/shard_map/pallas_call | solution.py:219
  57.3 1.0 %copy.9 = f32[2048,128]{1,0:T(8,128)} copy(f32[2048,128]{1,0:T(8,128)S(1)} %get-tuple-element.4) | data formatting | bytes 2097152
  58.3 0.6 %copy.10 = f32[128,128]{1,0:T(8,128)} copy(f32[128,128]{1,0:T(8,128)S(1)} %get-tuple-element.5) | data formatting | bytes 131072
Async XLA Ops:
  0.6 1.0 %copy-start = (bf16[2048,128]{1,0:T(8,128)(2,1)S(1)}, bf16[2048,128]{1,0:T(8,128)(2,1)}, u32[]{:S(2)}) copy-start(bf16[2048,128]{1,0:T(8,128)(2,1)} %param.9) | copy-start | bytes 1572868
  1.7 0.7 %copy-start.1 = (s32[16,16]{1,0:T(8,128)S(1)}, s32[16,16]{1,0:T(8,128)}, u32[]{:S(2)}) copy-start(s32[16,16]{1,0:T(8,128)} %cols_ref.1) | copy-start | bytes 3076
  2.4 0.7 %copy-start.2 = (s32[16]{0:T(128)S(1)}, s32[16]{0:T(128)}, u32[]{:S(2)}) copy-start(s32[16]{0:T(128)} %live_ref.1) | copy-start | bytes 196
  3.0 0.7 %copy-start.3 = (f32[16]{0:T(128)S(1)}, f32[16]{0:T(128)}, u32[]{:S(2)}) copy-start(f32[16]{0:T(128)} %visc_ref.1) | copy-start | bytes 196

commit v2 on v1

--- a/solution.py
+++ b/solution.py
@@ -18,6 +18,7 @@
 LINE = 16
 PLANE = 16
 SUB = 8
+CHUNK = 256
 DEAD = 3 * BLOCKS
 
 
@@ -81,9 +82,9 @@
 
 
 def kernel(
-    cols_ref, live_ref, visc_ref, op_hbm, sketch_hbm, basis_hbm, tri_ref,
-    ops, window, image, gram, part, recv1, recv2, total, inverse, out,
-    op_sems, own_sem, out_sems, halo_send, halo_recv, send_sems, recv_sems,
+    cols_hbm, live_hbm, visc_hbm, op_hbm, sketch_hbm, hi_ref, mid_ref, low_ref, tri_ref, inverse,
+    cols_ref, live_ref, visc_ref, ops, window, image, gram, part, recv1, recv2, total,
+    small_sems, op_sems, own_sem, halo_send, halo_recv, send_sems, recv_sems,
 ):
     z, row = lax.axis_index("grp"), lax.axis_index("row")
     core = lax.rem(row, 2)
@@ -91,7 +92,11 @@
     me = z * ROW + row
     mine = 2 * z + core
 
-    loads = []
+    loads = [
+        pltpu.make_async_copy(cols_hbm, cols_ref, small_sems.at[0]),
+        pltpu.make_async_copy(live_hbm, live_ref, small_sems.at[1]),
+        pltpu.make_async_copy(visc_hbm, visc_ref, small_sems.at[2]),
+    ]
     for r in range(BLOCKS):
         loads.append(pltpu.make_async_copy(op_hbm.at[r], ops.at[r], op_sems.at[r]))
     own = pltpu.make_async_copy(sketch_hbm, window.at[pl.ds(BLOCKS, BLOCKS)], own_sem)
@@ -146,16 +151,21 @@
             acc = acc + jnp.dot(lhs, rhs, preferred_element_type=F32)
         img = acc * visc_ref[r]
         image[pl.ds(pl.multiple_of(r * B, B), B), :] = img
-        hi, mid, low = split3(img)
+        return 0
+
+    lax.fori_loop(0, BLOCKS, block_row, 0, unroll=4)
+    for at in range(0, BLOCKS * B, CHUNK):
+        rows_at = slice(at, at + CHUNK)
+        hi, mid, low = split3(image[rows_at, :])
+        hi_ref[rows_at, :] = hi
+        mid_ref[rows_at, :] = mid
+        low_ref[rows_at, :] = low
         first = lax.dot_general(
             hi, jnp.concatenate([hi, mid, low], axis=1), (((0,), (0,)), ((), ())), preferred_element_type=F32
         )
         second = lax.dot_general(mid, mid, (((0,), (0,)), ((), ())), preferred_element_type=F32)
         gram[:, 0:K] += first[:, 0:K] + second
         gram[:, K : 2 * K] += first[:, K : 2 * K] + first[:, 2 * K :]
-        return 0
-
-    lax.fori_loop(0, BLOCKS, block_row, 0)
     cross = gram[:, K : 2 * K]
     local = gram[:, 0:K] + (cross + cross.T)
     part[...] = local.reshape(LINE, SUB, K)
@@ -193,35 +203,45 @@
     scale = 1.0 / (NDEV * BLOCKS * B)
     factor([total[q] * scale for q in range(K // SUB)], tri_ref, inverse)
 
+    for c in copies:
+        c.wait_send()
+
+
+def basis_kernel(hi_ref, mid_ref, low_ref, tri, inverse, basis_hbm, tri_hbm, out, out_sems, tri_sem):
+    tri_copy = pltpu.make_async_copy(tri, tri_hbm, tri_sem)
+    tri_copy.start()
     whi, wmid, wlow = split3(inverse[...])
     weights = jnp.concatenate([whi, whi, wmid, whi, wmid, wlow], axis=1)
 
     def basis_row(r, _):
         at = pl.ds(pl.multiple_of(r * B, B), B)
-        hi, mid, low = split3(image[at, :])
+        hi, mid, low = hi_ref[at, :], mid_ref[at, :], low_ref[at, :]
         lhs = jnp.concatenate([hi, mid, hi, low, mid, hi], axis=1)
         out[at, :] = lax.dot_general(lhs, weights, (((1,), (1,)), ((), ())), preferred_element_type=F32)
         pltpu.make_async_copy(out.at[at], basis_hbm.at[at], out_sems.at[r]).start()
         return 0
 
-    lax.fori_loop(0, BLOCKS, basis_row, 0)
+    lax.fori_loop(0, BLOCKS, basis_row, 0, unroll=16)
     for r in range(BLOCKS):
         at = pl.ds(r * B, B)
         pltpu.make_async_copy(out.at[at], basis_hbm.at[at], out_sems.at[r]).wait()
-    for c in copies:
-        c.wait_send()
+    tri_copy.wait()
 
 
 def shards(operator, columns, live_blocks, viscosity, sketch):
     rows_dev = BLOCKS * B
-    smem = pl.BlockSpec(memory_space=pltpu.SMEM)
-    hbm = pl.BlockSpec(memory_space=pl.ANY)
-    return pl.pallas_call(
+    vmem = pl.BlockSpec(memory_space=pltpu.VMEM)
+    hbm = pl.BlockSpec(memory_space=pltpu.HBM)
+    args = (columns, live_blocks, viscosity, operator, sketch.reshape(BLOCKS, B, K))
+    *parts, triangle, inverse = pl.pallas_call(
         kernel,
-        out_shape=[jax.ShapeDtypeStruct((rows_dev, K), F32), jax.ShapeDtypeStruct((K, K), F32)],
-        in_specs=[smem, smem, smem, hbm, hbm],
-        out_specs=[hbm, pl.BlockSpec(memory_space=pltpu.VMEM)],
+        out_shape=[pltpu.VMEM((rows_dev, K), BF16)] * 3 + [pltpu.VMEM((K, K), F32)] * 2,
+        in_specs=[hbm] * 5,
+        out_specs=[vmem] * 5,
         scratch_shapes=[
+            pltpu.SMEM((BLOCKS, SLOTS), jnp.int32),
+            pltpu.SMEM((BLOCKS,), jnp.int32),
+            pltpu.SMEM((BLOCKS,), F32),
             pltpu.VMEM((BLOCKS, SLOTS, B, B), BF16),
             pltpu.VMEM((3 * BLOCKS + 1, B, K), BF16),
             pltpu.VMEM((rows_dev, K), F32),
@@ -230,21 +250,32 @@
             pltpu.VMEM((LINE, SUB, K), F32),
             pltpu.VMEM((PLANE, SUB, K), F32),
             pltpu.VMEM((LINE, SUB, K), F32),
-            pltpu.VMEM((K, K), F32),
-            pltpu.VMEM((rows_dev, K), F32),
+            pltpu.SemaphoreType.DMA((3,)),
             pltpu.SemaphoreType.DMA((BLOCKS,)),
             pltpu.SemaphoreType.DMA,
-            pltpu.SemaphoreType.DMA((BLOCKS,)),
             pltpu.SemaphoreType.DMA((2,)),
             pltpu.SemaphoreType.DMA((2,)),
             pltpu.SemaphoreType.DMA((3, LINE)),
             pltpu.SemaphoreType.DMA((3, LINE)),
         ],
         compiler_params=pltpu.CompilerParams(
-            collective_id=0, has_side_effects=True, vmem_limit_bytes=48 * 2**20
+            collective_id=0, has_side_effects=True, vmem_limit_bytes=40 * 2**20
         ),
         cost_estimate=pl.CostEstimate(flops=1_300_000_000, bytes_accessed=11_000_000, transcendentals=0),
-    )(columns, live_blocks, viscosity, operator, sketch.reshape(BLOCKS, B, K))
+    )(*[pltpu.with_memory_space_constraint(x, pltpu.HBM) for x in args])
+    return pl.pallas_call(
+        basis_kernel,
+        out_shape=[jax.ShapeDtypeStruct((rows_dev, K), F32), jax.ShapeDtypeStruct((K, K), F32)],
+        in_specs=[vmem] * 5,
+        out_specs=[hbm] * 2,
+        scratch_shapes=[
+            pltpu.VMEM((rows_dev, K), F32),
+            pltpu.SemaphoreType.DMA((BLOCKS,)),
+            pltpu.SemaphoreType.DMA,
+        ],
+        compiler_params=pltpu.CompilerParams(vmem_limit_bytes=16 * 2**20),
+        cost_estimate=pl.CostEstimate(flops=200_000_000, bytes_accessed=2_100_000, transcendentals=0),
+    )(*[pltpu.with_memory_space_constraint(x, pltpu.VMEM) for x in (*parts, triangle, inverse)])
 
 
 def solution(mesh):

time: 59.1 us -> 46.5 us (0.79)
  Pallas kernels: 53.6 us -> 45.8 us
  local copies, waits for them, and re-layouts: 4.64 us -> 0 us
    pallas_call x1 -> x2, Pallas kernels: 53.6 us -> 45.8 us  [the longest x1 44 us: shards(): pl.pallas_call(kernel, out_shape=[pltpu.VMEM((rows_dev, K), BF16)] * 3 +...]
    unnamed x10 -> x0, local copies, waits for them, and re-layouts: 4.64 us -> none
where the time goes in v2:
time: 46.5 us; the launch traced here: 46.4 us
  Pallas kernels  45.8 us (98%)
  between operations  0.64 us (1%)
    pallas_call x1, Pallas kernels, shards(): pl.pallas_call(kernel, out_shape=[pltpu.VMEM((rows_dev, K), BF16)] * 3 +...  44 us
    pallas_call x1, Pallas kernels, shards(): pl.pallas_call(basis_kernel, out_shape=[jax.ShapeDtypeStruct((rows_dev, K...  1.79 us

profile of v2, /device:TPU:1, one launch (start us, length us, event | category | flops | bytes accessed | tf_op | source)
XLA Modules:
  0.0 46.4 jit_solution(3723869093010782330)
XLA Ops:
  0.6 44.0 %shard_map.68 = (bf16[2048,128]{1,0:T(8,128)(2,1)S(1)}, bf16[2048,128]{1,0:T(8,128)(2,1)S(1)}, bf16[2048,128]{1,0:T(8,128)(2,1)S(1)}, f32[128,128]{1,0:T(8,128)S(1)}, f32[128,128]{1,0:T(8,128)S(1)}) custom-call(s32[16,16]{1,0:T(8,128)} %cols_hbm.1, s32[16]{0:T(128)} %live_hbm.1, f32[16]{0:T(128)} %visc_hbm.1, bf16[16,16,128,128]{3,2,1,0:T(8,128)(2,1)} %op_hbm.1, ...), custom_call_target="tpu_custom_call" | custom-call | flops 1300000000 | bytes 11000000 | tf_op jit(solution)/shard_map/pallas_call | solution.py:236
  44.6 1.8 %shard_map.69 = (f32[2048,128]{1,0:T(8,128)}, f32[128,128]{1,0:T(8,128)}) custom-call(bf16[2048,128]{1,0:T(8,128)(2,1)S(1)} %get-tuple-element.7.hi_ref, bf16[2048,128]{1,0:T(8,128)(2,1)S(1)} %get-tuple-element.8.mid_ref, bf16[2048,128]{1,0:T(8,128)(2,1)S(1)} %get-tuple-element.9.low_ref, f32[128,128]{1,0:T(8,128)S(1)} %get-tuple-element.10.tri, ...), custom_call_target="tpu_custom_call" | custom-call | flops 200000000 | bytes 2100000 | tf_op jit(solution)/shard_map/pallas_call | solution.py:266

commit v3 on v2

--- a/solution.py
+++ b/solution.py
@@ -19,6 +19,7 @@
 PLANE = 16
 SUB = 8
 CHUNK = 256
+NEAR = 2
 DEAD = 3 * BLOCKS
 
 
@@ -32,22 +33,35 @@
     return jnp.broadcast_to(v[:, c : c + 1], (SUB, K))
 
 
-def rows(v, i):
-    return jnp.broadcast_to(v[i : i + 1, :], (SUB, K))
-
-
-def factor(gram, tri_ref, inv_ref):
+def factor(gram, work, tri_ref, inv_ref):
     lane = lax.broadcasted_iota(jnp.int32, (SUB, K), 1)
     sub = lax.broadcasted_iota(jnp.int32, (SUB, K), 0)
     n = K // SUB
+
+    def pack(v):
+        block = v[0]
+        for k in range(1, SUB):
+            block = jnp.where(sub == k, v[k], block)
+        return block
+
     a = list(gram)
     x = [jnp.where(lane == sub + SUB * q, 1.0, 0.0).astype(F32) for q in range(n)]
     for p in range(n):
         o = SUB * p
-        col = {q: [lanes(a[q], o + k) for k in range(SUB)] for q in range(p, n)}
-        diag = [[rows(col[p][j], i) if j <= i else None for j in range(SUB)] for i in range(SUB)]
-        ra = [rows(a[p], i) for i in range(SUB)]
-        rx = [rows(x[p], i) for i in range(SUB)]
+        near = list(range(p + 1, min(p + 1 + NEAR, n)))
+        col = {q: [lanes(a[q], o + k) for k in range(SUB)] for q in (p, *near)}
+        at = (p % 2) * 10 * SUB
+        work[at : at + SUB, :] = a[p]
+        work[at + SUB : at + 2 * SUB, :] = x[p]
+        for j in range(SUB):
+            work[at + (2 + j) * SUB : at + (3 + j) * SUB, :] = col[p][j]
+
+        def spread(r):
+            return jnp.broadcast_to(work[at + r : at + r + 1, :], (SUB, K))
+
+        diag = [[spread((2 + j) * SUB + i) if j <= i else None for j in range(SUB)] for i in range(SUB)]
+        ra = [spread(i) for i in range(SUB)]
+        rx = [spread(SUB + i) for i in range(SUB)]
         inv = [None] * SUB
         for k in range(SUB):
             inv[k] = 1.0 / diag[k][k]
@@ -58,19 +72,30 @@
             for i in range(k + 1, SUB):
                 ra[i] = ra[i] - mult[i] * ra[k]
                 rx[i] = rx[i] - mult[i] * rx[k]
-            for q in range(p + 1, n):
+            for q in near:
                 for i in range(k + 1, SUB):
                     col[q][i] = col[q][i] - mult[i] * col[q][k]
-        for i in range(SUB):
-            root = lax.rsqrt(diag[i][i])
-            tri_ref[o + i : o + i + 1, :] = jnp.where(lane >= o + i, ra[i] * root, 0.0)[0:1]
-            inv_ref[o + i : o + i + 1, :] = (rx[i] * root)[0:1]
+        pa, px = pack(ra), pack(rx)
+        root = lax.rsqrt(pack([diag[i][i] for i in range(SUB)]))
+        tri_ref[o : o + SUB, :] = jnp.where(lane >= sub + o, pa * root, 0.0)
+        inv_ref[o : o + SUB, :] = px * root
         ga = [ra[i] * inv[i] for i in range(SUB)]
         gx = [rx[i] * inv[i] for i in range(SUB)]
-        for q in range(p + 1, n):
+        for q in near:
             for k in range(SUB):
                 a[q] = a[q] - col[q][k] * ga[k]
                 x[q] = x[q] - col[q][k] * gx[k]
+        if p + 1 + NEAR < n:
+            pi = pack(inv)
+            h, m, w = split3(pa)
+            gh, gm, gw = split3(jnp.concatenate([pa * pi, px * pi], axis=1))
+            lhs = jnp.concatenate([v.astype(F32) for v in (h, h, m, h, w, m)], axis=0).astype(BF16)
+            rhs = jnp.concatenate([v.astype(F32) for v in (gh, gm, gh, gw, gh, gm)], axis=0).astype(BF16)
+            off = lax.dot_general(lhs, rhs, (((0,), (0,)), ((), ())), preferred_element_type=F32)
+            for q in range(p + 1 + NEAR, n):
+                da = off[SUB * q : SUB * (q + 1), 0:K]
+                a[q] = a[q] - da
+                x[q] = x[q] - off[SUB * q : SUB * (q + 1), K : 2 * K]
 
 
 def split3(v):
@@ -83,7 +108,7 @@
 
 def kernel(
     cols_hbm, live_hbm, visc_hbm, op_hbm, sketch_hbm, hi_ref, mid_ref, low_ref, tri_ref, inverse,
-    cols_ref, live_ref, visc_ref, ops, window, image, gram, part, recv1, recv2, total,
+    cols_ref, live_ref, visc_ref, ops, window, image, gram, part, recv1, recv2, total, work,
     small_sems, op_sems, own_sem, halo_send, halo_recv, send_sems, recv_sems,
 ):
     z, row = lax.axis_index("grp"), lax.axis_index("row")
@@ -91,7 +116,6 @@
     chip = row // 2
     me = z * ROW + row
     mine = 2 * z + core
-
     loads = [
         pltpu.make_async_copy(cols_hbm, cols_ref, small_sems.at[0]),
         pltpu.make_async_copy(live_hbm, live_ref, small_sems.at[1]),
@@ -153,7 +177,7 @@
         image[pl.ds(pl.multiple_of(r * B, B), B), :] = img
         return 0
 
-    lax.fori_loop(0, BLOCKS, block_row, 0, unroll=4)
+    lax.fori_loop(0, BLOCKS, block_row, 0, unroll=8)
     for at in range(0, BLOCKS * B, CHUNK):
         rows_at = slice(at, at + CHUNK)
         hi, mid, low = split3(image[rows_at, :])
@@ -196,13 +220,13 @@
         c = remote(total.at[mine], total.at[mine], send_sems.at[2, other], recv_sems.at[2, mine], dev)
         c.start()
         copies.append(c)
+    scale = 1.0 / (NDEV * BLOCKS * B)
+
     for k in order:
         other, dev = line_peer(k)
         remote(total.at[other], total.at[other], send_sems.at[2, other], recv_sems.at[2, other], dev).wait_recv()
 
-    scale = 1.0 / (NDEV * BLOCKS * B)
-    factor([total[q] * scale for q in range(K // SUB)], tri_ref, inverse)
-
+    factor([total[q] * scale for q in range(K // SUB)], work, tri_ref, inverse)
     for c in copies:
         c.wait_send()
 
@@ -250,6 +274,7 @@
             pltpu.VMEM((LINE, SUB, K), F32),
             pltpu.VMEM((PLANE, SUB, K), F32),
             pltpu.VMEM((LINE, SUB, K), F32),
+            pltpu.VMEM((20 * SUB, K), F32),
             pltpu.SemaphoreType.DMA((3,)),
             pltpu.SemaphoreType.DMA((BLOCKS,)),
             pltpu.SemaphoreType.DMA,

time: 46.5 us -> 44.6 us (0.959)
  Pallas kernels: 45.8 us -> 43.8 us
    pallas_call x1, Pallas kernels: 44 us -> 42 us  [shards(): pl.pallas_call(kernel, out_shape=[pltpu.VMEM((rows_dev, K), BF16)] * 3 +...]
where the time goes in v3:
time: 44.6 us; the launch traced here: 44.5 us
  Pallas kernels  43.8 us (98%)
  between operations  0.64 us (1%)
    pallas_call x1, Pallas kernels, shards(): pl.pallas_call(kernel, out_shape=[pltpu.VMEM((rows_dev, K), BF16)] * 3 +...  42 us
    pallas_call x1, Pallas kernels, shards(): pl.pallas_call(basis_kernel, out_shape=[jax.ShapeDtypeStruct((rows_dev, K...  1.79 us

profile of v3, /device:TPU:1, one launch (start us, length us, event | category | flops | bytes accessed | tf_op | source)
XLA Modules:
  0.0 44.5 jit_solution(10256746747010456345)
XLA Ops:
  0.6 42.0 %shard_map.68 = (bf16[2048,128]{1,0:T(8,128)(2,1)S(1)}, bf16[2048,128]{1,0:T(8,128)(2,1)S(1)}, bf16[2048,128]{1,0:T(8,128)(2,1)S(1)}, f32[128,128]{1,0:T(8,128)S(1)}, f32[128,128]{1,0:T(8,128)S(1)}) custom-call(s32[16,16]{1,0:T(8,128)} %cols_hbm.1, s32[16]{0:T(128)} %live_hbm.1, f32[16]{0:T(128)} %visc_hbm.1, bf16[16,16,128,128]{3,2,1,0:T(8,128)(2,1)} %op_hbm.1, ...), custom_call_target="tpu_custom_call" | custom-call | flops 1300000000 | bytes 11000000 | tf_op jit(solution)/shard_map/pallas_call | solution.py:260
  42.7 1.8 %shard_map.69 = (f32[2048,128]{1,0:T(8,128)}, f32[128,128]{1,0:T(8,128)}) custom-call(bf16[2048,128]{1,0:T(8,128)(2,1)S(1)} %get-tuple-element.7.hi_ref, bf16[2048,128]{1,0:T(8,128)(2,1)S(1)} %get-tuple-element.8.mid_ref, bf16[2048,128]{1,0:T(8,128)(2,1)S(1)} %get-tuple-element.9.low_ref, f32[128,128]{1,0:T(8,128)S(1)} %get-tuple-element.10.tri, ...), custom_call_target="tpu_custom_call" | custom-call | flops 200000000 | bytes 2100000 | tf_op jit(solution)/shard_map/pallas_call | solution.py:291

commit v4 on v3

--- a/solution.py
+++ b/solution.py
@@ -18,7 +18,7 @@
 LINE = 16
 PLANE = 16
 SUB = 8
-CHUNK = 256
+CHUNK = 512
 NEAR = 2
 DEAD = 3 * BLOCKS
 
@@ -108,7 +108,7 @@
 
 def kernel(
     cols_hbm, live_hbm, visc_hbm, op_hbm, sketch_hbm, hi_ref, mid_ref, low_ref, tri_ref, inverse,
-    cols_ref, live_ref, visc_ref, ops, window, image, gram, part, recv1, recv2, total, work,
+    cols_ref, live_ref, visc_ref, ops, window, gram, part, recv1, recv2, total, work,
     small_sems, op_sems, own_sem, halo_send, halo_recv, send_sems, recv_sems,
 ):
     z, row = lax.axis_index("grp"), lax.axis_index("row")
@@ -125,6 +125,10 @@
         loads.append(pltpu.make_async_copy(op_hbm.at[r], ops.at[r], op_sems.at[r]))
     own = pltpu.make_async_copy(sketch_hbm, window.at[pl.ds(BLOCKS, BLOCKS)], own_sem)
 
+    def arrived(buf, phase):
+        others = buf.at[pl.ds(0, LINE - 1)]
+        pltpu.make_async_copy(others, others, recv_sems.at[phase]).wait()
+
     def line_peer(k):
         other = lax.rem(mine + k, LINE)
         return other, (other // 2, row - core + lax.rem(other, 2))
@@ -149,13 +153,14 @@
     window[DEAD] = jnp.zeros((B, K), BF16)
     pl.semaphore_wait(barrier, len(peers))
 
+    own.wait()
+    block = window.at[pl.ds(BLOCKS, BLOCKS)]
     halo = [
-        remote(sketch_hbm, window.at[pl.ds(0, BLOCKS)], halo_send.at[0], halo_recv.at[0], up_dev),
-        remote(sketch_hbm, window.at[pl.ds(2 * BLOCKS, BLOCKS)], halo_send.at[1], halo_recv.at[1], down_dev),
+        remote(block, window.at[pl.ds(0, BLOCKS)], halo_send.at[0], halo_recv.at[0], up_dev),
+        remote(block, window.at[pl.ds(2 * BLOCKS, BLOCKS)], halo_send.at[1], halo_recv.at[1], down_dev),
     ]
     for c in halo:
         c.start()
-    own.wait()
     for c in loads:
         c.wait()
     for c in halo:
@@ -174,16 +179,14 @@
             rhs = jnp.concatenate([window[i0], window[i1]], axis=0)
             acc = acc + jnp.dot(lhs, rhs, preferred_element_type=F32)
         img = acc * visc_ref[r]
-        image[pl.ds(pl.multiple_of(r * B, B), B), :] = img
+        at = pl.ds(pl.multiple_of(r * B, B), B)
+        hi_ref[at, :], mid_ref[at, :], low_ref[at, :] = split3(img)
         return 0
 
-    lax.fori_loop(0, BLOCKS, block_row, 0, unroll=8)
+    lax.fori_loop(0, BLOCKS, block_row, 0, unroll=16)
     for at in range(0, BLOCKS * B, CHUNK):
         rows_at = slice(at, at + CHUNK)
-        hi, mid, low = split3(image[rows_at, :])
-        hi_ref[rows_at, :] = hi
-        mid_ref[rows_at, :] = mid
-        low_ref[rows_at, :] = low
+        hi, mid, low = hi_ref[rows_at, :], mid_ref[rows_at, :], low_ref[rows_at, :]
         first = lax.dot_general(
             hi, jnp.concatenate([hi, mid, low], axis=1), (((0,), (0,)), ((), ())), preferred_element_type=F32
         )
@@ -198,40 +201,40 @@
     copies = []
     for k in order:
         other, dev = line_peer(k)
-        c = remote(part.at[other], recv1.at[mine], send_sems.at[0, other], recv_sems.at[0, mine], dev)
+        c = remote(part.at[other], recv1.at[mine], send_sems.at[0, other], recv_sems.at[0], dev)
         c.start()
         copies.append(c)
+    for c in copies:
+        c.wait_send()
+    arrived(recv1, 0)
+    mine_sum = jnp.sum(recv1[...], axis=0)
+    recv2[chip] = mine_sum
+    copies = []
+    for k in order:
+        other, dev = plane_peer(k)
+        c = remote(recv2.at[chip], recv2.at[chip], send_sems.at[1, other], recv_sems.at[1], dev)
+        c.start()
+        copies.append(c)
+    for c in copies:
+        c.wait_send()
+    arrived(recv2, 1)
+    total[mine] = jnp.sum(recv2[...], axis=0)
+    copies = []
     for k in order:
         other, dev = line_peer(k)
-        remote(part.at[other], recv1.at[other], send_sems.at[0, other], recv_sems.at[0, other], dev).wait_recv()
-    mine_sum = jnp.sum(recv1[...], axis=0)
-    recv2[chip] = mine_sum
-    for k in order:
-        other, dev = plane_peer(k)
-        c = remote(recv2.at[chip], recv2.at[chip], send_sems.at[1, other], recv_sems.at[1, chip], dev)
-        c.start()
-        copies.append(c)
-    for k in order:
-        other, dev = plane_peer(k)
-        remote(recv2.at[other], recv2.at[other], send_sems.at[1, other], recv_sems.at[1, other], dev).wait_recv()
-    total[mine] = jnp.sum(recv2[...], axis=0)
-    for k in order:
-        other, dev = line_peer(k)
-        c = remote(total.at[mine], total.at[mine], send_sems.at[2, other], recv_sems.at[2, mine], dev)
+        c = remote(total.at[mine], total.at[mine], send_sems.at[2, other], recv_sems.at[2], dev)
         c.start()
         copies.append(c)
     scale = 1.0 / (NDEV * BLOCKS * B)
 
-    for k in order:
-        other, dev = line_peer(k)
-        remote(total.at[other], total.at[other], send_sems.at[2, other], recv_sems.at[2, other], dev).wait_recv()
-
-    factor([total[q] * scale for q in range(K // SUB)], work, tri_ref, inverse)
     for c in copies:
         c.wait_send()
-
-
-def basis_kernel(hi_ref, mid_ref, low_ref, tri, inverse, basis_hbm, tri_hbm, out, out_sems, tri_sem):
+    arrived(total, 2)
+
+    factor([total[q] * scale for q in range(K // SUB)], work, tri_ref, inverse)
+
+
+def basis_kernel(hi_ref, mid_ref, low_ref, tri, inverse, basis_hbm, tri_hbm, out, out_sem, tri_sem):
     tri_copy = pltpu.make_async_copy(tri, tri_hbm, tri_sem)
     tri_copy.start()
     whi, wmid, wlow = split3(inverse[...])
@@ -242,13 +245,11 @@
         hi, mid, low = hi_ref[at, :], mid_ref[at, :], low_ref[at, :]
         lhs = jnp.concatenate([hi, mid, hi, low, mid, hi], axis=1)
         out[at, :] = lax.dot_general(lhs, weights, (((1,), (1,)), ((), ())), preferred_element_type=F32)
-        pltpu.make_async_copy(out.at[at], basis_hbm.at[at], out_sems.at[r]).start()
+        pltpu.make_async_copy(out.at[at], basis_hbm.at[at], out_sem).start()
         return 0
 
     lax.fori_loop(0, BLOCKS, basis_row, 0, unroll=16)
-    for r in range(BLOCKS):
-        at = pl.ds(r * B, B)
-        pltpu.make_async_copy(out.at[at], basis_hbm.at[at], out_sems.at[r]).wait()
+    pltpu.make_async_copy(out, basis_hbm, out_sem).wait()
     tri_copy.wait()
 
 
@@ -268,7 +269,6 @@
             pltpu.SMEM((BLOCKS,), F32),
             pltpu.VMEM((BLOCKS, SLOTS, B, B), BF16),
             pltpu.VMEM((3 * BLOCKS + 1, B, K), BF16),
-            pltpu.VMEM((rows_dev, K), F32),
             pltpu.VMEM((K, 2 * K), F32),
             pltpu.VMEM((LINE, SUB, K), F32),
             pltpu.VMEM((LINE, SUB, K), F32),
@@ -281,7 +281,7 @@
             pltpu.SemaphoreType.DMA((2,)),
             pltpu.SemaphoreType.DMA((2,)),
             pltpu.SemaphoreType.DMA((3, LINE)),
-            pltpu.SemaphoreType.DMA((3, LINE)),
+            pltpu.SemaphoreType.DMA((3,)),
         ],
         compiler_params=pltpu.CompilerParams(
             collective_id=0, has_side_effects=True, vmem_limit_bytes=40 * 2**20
@@ -295,7 +295,7 @@
         out_specs=[hbm] * 2,
         scratch_shapes=[
             pltpu.VMEM((rows_dev, K), F32),
-            pltpu.SemaphoreType.DMA((BLOCKS,)),
+            pltpu.SemaphoreType.DMA,
             pltpu.SemaphoreType.DMA,
         ],
         compiler_params=pltpu.CompilerParams(vmem_limit_bytes=16 * 2**20),

time: 44.6 us -> 43.4 us (0.973)
  Pallas kernels: 43.8 us -> 42.7 us
    pallas_call x1, Pallas kernels: 42 us -> 41.1 us  [shards(): pl.pallas_call(kernel, out_shape=[pltpu.VMEM((rows_dev, K), BF16)] * 3 +...]
where the time goes in v4:
time: 43.4 us
  Pallas kernels  42.7 us (98%)
  between operations  0.64 us (1%)
    pallas_call x1, Pallas kernels, shards(): pl.pallas_call(kernel, out_shape=[pltpu.VMEM((rows_dev, K), BF16)] * 3 +...  41.1 us
    pallas_call x1, Pallas kernels, shards(): pl.pallas_call(basis_kernel, out_shape=[jax.ShapeDtypeStruct((rows_dev, K...  1.65 us

profile of v4, /device:TPU:1, one launch (start us, length us, event | category | flops | bytes accessed | tf_op | source)
XLA Modules:
  0.0 43.4 jit_solution(9316540478354383546)
XLA Ops:
  0.6 41.1 %shard_map.68 = (bf16[2048,128]{1,0:T(8,128)(2,1)S(1)}, bf16[2048,128]{1,0:T(8,128)(2,1)S(1)}, bf16[2048,128]{1,0:T(8,128)(2,1)S(1)}, f32[128,128]{1,0:T(8,128)S(1)}, f32[128,128]{1,0:T(8,128)S(1)}) custom-call(s32[16,16]{1,0:T(8,128)} %cols_hbm.1, s32[16]{0:T(128)} %live_hbm.1, f32[16]{0:T(128)} %visc_hbm.1, bf16[16,16,128,128]{3,2,1,0:T(8,128)(2,1)} %op_hbm.1, ...), custom_call_target="tpu_custom_call" | custom-call | flops 1300000000 | bytes 11000000 | tf_op jit(solution)/shard_map/pallas_call | solution.py:261
  41.7 1.6 %shard_map.69 = (f32[2048,128]{1,0:T(8,128)}, f32[128,128]{1,0:T(8,128)}) custom-call(bf16[2048,128]{1,0:T(8,128)(2,1)S(1)} %get-tuple-element.7.hi_ref, bf16[2048,128]{1,0:T(8,128)(2,1)S(1)} %get-tuple-element.8.mid_ref, bf16[2048,128]{1,0:T(8,128)(2,1)S(1)} %get-tuple-element.9.low_ref, f32[128,128]{1,0:T(8,128)S(1)} %get-tuple-element.10.tri, ...), custom_call_target="tpu_custom_call" | custom-call | flops 200000000 | bytes 2100000 | tf_op jit(solution)/shard_map/pallas_call | solution.py:291

commit v5 on v4

--- a/solution.py
+++ b/solution.py
@@ -155,10 +155,12 @@
 
     own.wait()
     block = window.at[pl.ds(BLOCKS, BLOCKS)]
-    halo = [
-        remote(block, window.at[pl.ds(0, BLOCKS)], halo_send.at[0], halo_recv.at[0], up_dev),
-        remote(block, window.at[pl.ds(2 * BLOCKS, BLOCKS)], halo_send.at[1], halo_recv.at[1], down_dev),
-    ]
+    halo = []
+    for side in (core, 1 - core):
+        slot = 1 - side
+        dev = tuple(jnp.where(side == 1, u, v) for u, v in zip(up_dev, down_dev))
+        there = window.at[pl.ds(pl.multiple_of(2 * BLOCKS * slot, BLOCKS), BLOCKS)]
+        halo.append(remote(block, there, halo_send.at[slot], halo_recv.at[slot], dev))
     for c in halo:
         c.start()
     for c in loads:
@@ -238,13 +240,20 @@
     tri_copy = pltpu.make_async_copy(tri, tri_hbm, tri_sem)
     tri_copy.start()
     whi, wmid, wlow = split3(inverse[...])
-    weights = jnp.concatenate([whi, whi, wmid, whi, wmid, wlow], axis=1)
+    large = jnp.concatenate([jnp.concatenate([whi, wmid], axis=1), jnp.concatenate([wmid, whi], axis=1)], axis=0)
+    small = jnp.concatenate([wlow, whi], axis=1)
+    rows_by_rows = (((1,), (1,)), ((), ()))
 
     def basis_row(r, _):
         at = pl.ds(pl.multiple_of(r * B, B), B)
         hi, mid, low = hi_ref[at, :], mid_ref[at, :], low_ref[at, :]
-        lhs = jnp.concatenate([hi, mid, hi, low, mid, hi], axis=1)
-        out[at, :] = lax.dot_general(lhs, weights, (((1,), (1,)), ((), ())), preferred_element_type=F32)
+        main = lax.dot_general(
+            jnp.concatenate([hi, mid], axis=1), large, rows_by_rows, preferred_element_type=F32
+        )
+        rest = lax.dot_general(
+            jnp.concatenate([hi, low], axis=1), small, rows_by_rows, preferred_element_type=F32
+        )
+        out[at, :] = main[:, 0:K] + (main[:, K : 2 * K] + rest)
         pltpu.make_async_copy(out.at[at], basis_hbm.at[at], out_sem).start()
         return 0
 

time: 43.4 us -> 43.4 us (level)
  no operation moved by 1% of the time
where the time goes in v5:
time: 43.4 us
  Pallas kernels  42.7 us (98%)
  between operations  0.64 us (1%)
    pallas_call x1, Pallas kernels, shards(): pl.pallas_call(kernel, out_shape=[pltpu.VMEM((rows_dev, K), BF16)] * 3 +...  41.1 us
    pallas_call x1, Pallas kernels, shards(): pl.pallas_call(basis_kernel, out_shape=[jax.ShapeDtypeStruct((rows_dev, K...  1.65 us

profile of v5, /device:TPU:1, one launch (start us, length us, event | category | flops | bytes accessed | tf_op | source)
XLA Modules:
  0.0 43.4 jit_solution(3120322283925708003)
XLA Ops:
  0.6 41.1 %shard_map.68 = (bf16[2048,128]{1,0:T(8,128)(2,1)S(1)}, bf16[2048,128]{1,0:T(8,128)(2,1)S(1)}, bf16[2048,128]{1,0:T(8,128)(2,1)S(1)}, f32[128,128]{1,0:T(8,128)S(1)}, f32[128,128]{1,0:T(8,128)S(1)}) custom-call(s32[16,16]{1,0:T(8,128)} %cols_hbm.1, s32[16]{0:T(128)} %live_hbm.1, f32[16]{0:T(128)} %visc_hbm.1, bf16[16,16,128,128]{3,2,1,0:T(8,128)(2,1)} %op_hbm.1, ...), custom_call_target="tpu_custom_call" | custom-call | flops 1300000000 | bytes 11000000 | tf_op jit(solution)/shard_map/pallas_call | solution.py:270
  41.7 1.6 %shard_map.69 = (f32[2048,128]{1,0:T(8,128)}, f32[128,128]{1,0:T(8,128)}) custom-call(bf16[2048,128]{1,0:T(8,128)(2,1)S(1)} %get-tuple-element.7.hi_ref, bf16[2048,128]{1,0:T(8,128)(2,1)S(1)} %get-tuple-element.8.mid_ref, bf16[2048,128]{1,0:T(8,128)(2,1)S(1)} %get-tuple-element.9.low_ref, f32[128,128]{1,0:T(8,128)S(1)} %get-tuple-element.10.tri, ...), custom_call_target="tpu_custom_call" | custom-call | flops 200000000 | bytes 2100000 | tf_op jit(solution)/shard_map/pallas_call | solution.py:300
